TPU v7x, 32 devices: a whole 2x2x4 slice. The times are simulated.
32 devices in a mesh: tile: 8 (over z, y), trc: 4 (over x, core).
Axes of the slice: x: 2, y: 2, z: 4, core: 2. Of those that a mesh axis runs over, the one named last changes fastest.
Arguments:
- tracer: float32 [8, 8, 16, 4096], P('trc', None, None, 'tile'), may hold values from -6 to 6
- met_blocks: bfloat16 [128, 16, 256], P('tile'), may hold values from -6 to 6
- intersection_list: int32 [8, 32], replicated, may hold values from -1 to 127, as said below
- entry_index: int32 [8, 16, 8], P('tile'), may hold values from 0 to 31, as said below
- weight_id: int32 [8, 16, 8], P('tile'), may hold values from 0 to 7
- weight_table: bfloat16 [8, 256, 512], replicated, may hold values from -0.125 to 0.125
Outputs:
- tracer_next: float32 [8, 8, 16, 4096], P('trc', None, None, 'tile')
- met_fields: float32 [2, 8, 16, 4096], P(None, None, None, 'tile')
Inputs may be any that keep to these rules, and one draw needn't show every extreme that they name: `intersection_list`: row t holds, for each source tile s in order, 4 slots: distinct ids of blocks owned by s (s * 16 to s * 16 + 15), used slots first, the rest -1. Each row has a source with all 4 slots used, the last source fills all its slots in every row, and each source has all 4 slots used in some row. `entry_index`: each entry names a used slot of its tile's list, and every used slot is named by some entry.
All inputs are finite; a program needn't handle non-finite values.
Results may differ from a plain program's by a relative error of at most 0.0003.
Values may be sent and summed in bfloat16 or wider, within the bound.
A program may use at most 64 MiB of HBM per device.

v0:
```python
import jax
import jax.numpy as jnp
from jax import lax
from jax.sharding import PartitionSpec as P


def padded(cells, sides, width):
    for axis, dim in sides:
        count = lax.axis_size(axis)
        head = lax.slice_in_dim(cells, 0, width, axis=dim)
        tail = lax.slice_in_dim(cells, cells.shape[dim] - width, cells.shape[dim], axis=dim)
        cells = jnp.concatenate(
            [
                lax.ppermute(tail, axis, [(i, (i + 1) % count) for i in range(count)]),
                cells,
                lax.ppermute(head, axis, [((i + 1) % count, i) for i in range(count)]),
            ],
            axis=dim,
        )
    return cells


def ppm_substep(tracer_ext, courant, massflux):
    face_values = 7.0 / 12.0 * (tracer_ext[..., 1:-2] + tracer_ext[..., 2:-1]) - 1.0 / 12.0 * (
        tracer_ext[..., :-3] + tracer_ext[..., 3:]
    )
    left_edge = face_values[..., :-1]
    right_edge = face_values[..., 1:]
    centers = tracer_ext[..., 2:-2]
    slopes = right_edge - left_edge
    curvature = 6.0 * centers - 3.0 * (left_edge + right_edge)
    face_courant = courant[..., 3:-2]
    face_mass = massflux[..., 3:-2]
    upwind_abs = jnp.abs(face_courant)
    shape_factor = 1.0 - upwind_abs * (2.0 / 3.0)
    from_left = right_edge[..., :-1] - 0.5 * upwind_abs * (
        slopes[..., :-1] - shape_factor * curvature[..., :-1]
    )
    from_right = left_edge[..., 1:] + 0.5 * upwind_abs * (
        slopes[..., 1:] + shape_factor * curvature[..., 1:]
    )
    crossing = jnp.where(face_courant > 0, from_left, from_right)
    fluxes = face_courant * face_mass * crossing
    return tracer_ext[..., 3:-3] - (fluxes[..., 1:] - fluxes[..., :-1])


def pack_blocks(blocks, columns, tile_index):
    block_count = blocks.shape[0]
    local_ids = jnp.clip(columns - tile_index * block_count, 0, block_count - 1)
    picked = jnp.take(blocks, local_ids.reshape(-1), axis=0)
    picked = picked.reshape(columns.shape + blocks.shape[1:])
    return jnp.where((columns >= 0)[:, :, None, None], picked, jnp.zeros((), blocks.dtype))


def regrid_rows(arrived, entry_index, weight_id, weight_table):
    entries = arrived.reshape((-1,) + arrived.shape[2:])
    row_count = entry_index.shape[1]
    intersection_depth = entry_index.shape[2]
    field_rows = entries.shape[1]
    cells = entries.shape[2]
    block_kinds = weight_table.shape[0]
    sources = jnp.take(entries, entry_index[0].reshape(-1), axis=0)
    sources = sources.reshape(row_count, intersection_depth, field_rows, cells)
    kinds = lax.broadcasted_iota(jnp.int32, (row_count, intersection_depth, block_kinds), 2)
    selector = (weight_id[0][:, :, None] == kinds).astype(jnp.bfloat16)
    binned = jnp.einsum("ykw,ykfb->fywb", selector, sources, preferred_element_type=jnp.float32)
    binned = binned.reshape(field_rows * row_count, block_kinds * cells)
    table = weight_table.reshape(block_kinds * cells, weight_table.shape[2]).astype(jnp.float32)
    result = jnp.dot(
        binned, table, preferred_element_type=jnp.float32, precision=lax.Precision.HIGHEST
    )
    return result.reshape(field_rows, row_count, weight_table.shape[2])


def local(tracer, met_blocks, intersection_list, entry_index, weight_id, weight_table):
    tile_index = lax.axis_index("tile")
    tile_count = lax.axis_size("tile")
    slot_count = intersection_list.shape[1] // tile_count
    columns = lax.dynamic_slice_in_dim(intersection_list, tile_index * slot_count, slot_count, 1)
    outgoing = pack_blocks(met_blocks, columns, tile_index)
    arrived = lax.all_to_all(outgoing, "tile", split_axis=0, concat_axis=0, tiled=True)
    raw_fields = regrid_rows(arrived, entry_index, weight_id, weight_table)
    levels = tracer.shape[1]
    raw_fields = raw_fields.reshape((2, levels) + raw_fields.shape[1:])
    courant = 0.5 * jnp.tanh(raw_fields[0])
    massflux = 1.0 + 0.5 * jnp.tanh(raw_fields[1])
    met_fields = jnp.stack([courant, massflux])
    species = tracer.shape[0]
    stacked = jnp.concatenate([tracer, met_fields], axis=0)
    widened = padded(stacked, (("tile", 3),), 3)
    wide_courant = widened[species]
    wide_mass = widened[species + 1]
    first_pass = ppm_substep(widened[:species], wide_courant, wide_mass)
    refilled = padded(first_pass, (("tile", 3),), 3)
    second_pass = ppm_substep(refilled, wide_courant, wide_mass)
    return (second_pass, met_fields)


def solution(mesh):
    return jax.shard_map(
        local,
        mesh=mesh,
        in_specs=(
            P("trc", None, None, "tile"),
            P("tile", None, None),
            P(),
            P("tile", None, None),
            P("tile", None, None),
            P(),
        ),
        out_specs=(P("trc", None, None, "tile"), P(None, None, None, "tile")),
        check_vma=False,
    )
```

profile of v0, /device:TPU:0, one launch (start us, length us, event | category | flops | bytes accessed | tf_op | source)
XLA Modules:
  0.0 52.6 jit_solution(15620900792840594807)
XLA Ops:
  0.6 0.0 copy-start
  0.6 0.0 copy-start.2
  0.7 0.0 copy-start.3
  0.7 0.9 %compare_and_fusion = (pred[8,4]{1,0:T(8,128)(4,1)S(1)}, s32[8,4]{1,0:T(8,128)S(1)}, pred[8,4]{1,0:T(8,128)(4,1)S(1)}) fusion(s32[]{:T(128)S(6)} %mul.135, s32[8,32]{1,0:T(8,128)} %param.8, s32[]{:T(128)S(6)} %select_n.59), kind=kLoop, calls=%fused_computation.77 | loop fusion | flops 288 | bytes 328 | tf_op jit(solution)/shard_map/jit(_take)/and | solution.py:50
  1.6 0.1 reshape.137
  1.7 1.5 %gather_fusion = bf16[32,16,256]{2,1,0:T(8,128)(2,1)S(1)} fusion(bf16[16,16,256]{2,1,0:T(8,128)(2,1)} %param.7, s32[1024]{0:T(1024)S(1)} %pad_clamp_fusion.1), kind=kCustom, calls=%fused_computation | custom fusion | bytes 524416 | tf_op jit(solution)/shard_map/jit(_take)/gather | solution.py:50
  3.2 0.8 %select_select_fusion = bf16[8,4,16,256]{3,2,1,0:T(8,128)(2,1)} fusion(bf16[8,4,16,256]{3,2,1,0:T(8,128)(2,1)S(1)} %bitcast.44, pred[8,4]{1,0:T(8,128)(4,1)S(1)} %get-tuple-element.2, pred[8,4]{1,0:T(8,128)(4,1)S(1)} %get-tuple-element.19), kind=kLoop, calls=%fused_computation.68 | loop fusion | flops 262144 | bytes 524352 | tf_op jit(solution)/shard_map/jit(_where)/select_n | solution.py:52
  4.0 7.3 %all-to-all-start = ((bf16[8,4,16,256]{3,2,1,0:T(8,128)(2,1)}), bf16[8,4,16,256]{3,2,1,0:T(8,128)(2,1)S(1)}, u32[]{:S(2)}, u32[]{:S(2)}) async-start(bf16[8,4,16,256]{3,2,1,0:T(8,128)(2,1)} %select_select_fusion), calls=%async_computation | async-start | bytes 524288 | tf_op jit(solution)/shard_map/all_to_all | solution.py:81
  11.3 0.0 copy-done.2
  11.3 0.1 copy.12
  11.4 0.1 copy.11
  11.5 0.0 copy-done.3
  11.5 0.1 copy.13
  11.5 0.1 reshape_squeeze.6
  11.6 8.6 %all-to-all-done = bf16[8,4,16,256]{3,2,1,0:T(8,128)(2,1)S(1)} async-done(((bf16[8,4,16,256]{3,2,1,0:T(8,128)(2,1)}), bf16[8,4,16,256]{3,2,1,0:T(8,128)(2,1)S(1)}, u32[]{:S(2)}, u32[]{:S(2)}) %all-to-all-start) | async-done | bytes 262176 | tf_op jit(solution)/shard_map/all_to_all | solution.py:81
  20.2 0.6 %gather_fusion.1 = bf16[128,16,256]{2,1,0:T(8,128)(2,1)S(1)} fusion(bf16[32,16,256]{2,1,0:T(8,128)(2,1)S(1)} %bitcast.34, s32[1024]{0:T(1024)S(1)} %pad_clamp_fusion), kind=kCustom, calls=%fused_computation.1 | custom fusion | bytes 2097664 | tf_op jit(solution)/shard_map/jit(_take)/gather | solution.py:62
  20.9 0.2 broadcast_select_fusion
  21.1 0.5 convolution_bitcast_fusion
  21.5 0.2 copy.15
  21.8 0.9 %copy.17 = f32[32,8,8,256]{3,1,2,0:T(8,128)S(1)} copy(f32[32,8,8,256]{3,2,1,0:T(8,128)S(1)} %bitcast.32) | data formatting | bytes 4194304
  22.7 0.0 copy-done
  22.7 1.8 %fusion.37 = f32[256,512]{1,0:T(8,128)S(1)} fusion(f32[256,2048]{1,0:T(8,128)S(1)} %bitcast.33, bf16[2048,512]{1,0:T(8,128)(2,1)S(1)} %bitcast.31), kind=kOutput, calls=%fused_computation.85 | convolution fusion | flops 3221225472 | bytes 4718592 | tf_op jit(solution)/shard_map/dot_general | solution.py:69
  24.5 0.0 copy-start.1
  24.5 0.1 fusion.30
  24.6 0.9 %copy-done.1 = f32[2,8,16,512]{3,2,1,0:T(8,128)S(1)} copy-done((f32[2,8,16,512]{3,2,1,0:T(8,128)S(1)}, f32[2,8,16,512]{3,2,1,0:T(8,128)}, u32[]{:S(2)}) %copy-start.1) | copy-done | bytes 524312
  25.6 0.1 pad_maximum_fusion.11
  25.7 1.5 %collective-permute-start = (f32[4,8,16,3]{3,2,1,0:T(8,128)S(1)}, f32[4,8,16,3]{3,2,1,0:T(8,128)S(1)}, u32[]{:S(2)}, u32[]{:S(2)}) collective-permute-start(f32[4,8,16,3]{3,2,1,0:T(8,128)S(1)} %get-tuple-element.6), channel_id=1, source_target_pairs={{0,4},{4,8},{8,12},{12,16},{16,20},{20,24},{24,28},{28,0},{1,5},{5... | collective-permute-start | bytes 18440 | tf_op jit(solution)/shard_map/ppermute | solution.py:14
  27.2 3.3 %collective-permute-start.1 = (f32[4,8,16,3]{3,2,1,0:T(8,128)S(1)}, f32[4,8,16,3]{3,2,1,0:T(8,128)S(1)}, u32[]{:S(2)}, u32[]{:S(2)}) collective-permute-start(f32[4,8,16,3]{3,2,1,0:T(8,128)S(1)} %get-tuple-element.7), channel_id=1, source_target_pairs={{4,0},{8,4},{12,8},{16,12},{20,16},{24,20},{28,24},{0,28},{5,1},{9... | collective-permute-start | bytes 18440 | tf_op jit(solution)/shard_map/ppermute | solution.py:16
  30.5 5.8 %collective-permute-done = f32[4,8,16,3]{3,2,1,0:T(8,128)S(1)} collective-permute-done((f32[4,8,16,3]{3,2,1,0:T(8,128)S(1)}, f32[4,8,16,3]{3,2,1,0:T(8,128)S(1)}, u32[]{:S(2)}, u32[]{:S(2)}) %collective-permute-start) | collective-permute-done | bytes 6176 | tf_op jit(solution)/shard_map/ppermute | solution.py:14
  36.2 2.2 %collective-permute-done.1 = f32[4,8,16,3]{3,2,1,0:T(8,128)S(1)} collective-permute-done((f32[4,8,16,3]{3,2,1,0:T(8,128)S(1)}, f32[4,8,16,3]{3,2,1,0:T(8,128)S(1)}, u32[]{:S(2)}, u32[]{:S(2)}) %collective-permute-start.1) | collective-permute-done | bytes 6176 | tf_op jit(solution)/shard_map/ppermute | solution.py:16
  38.4 0.5 pad_maximum_fusion
  39.0 0.6 %fusion.23 = f32[2,8,16,515]{3,2,1,0:T(8,128)S(1)} fusion(f32[4,8,16,3]{3,2,1,0:T(8,128)S(1)} %collective-permute-done.1, f32[1,8,16,512]{3,2,1,0:T(8,128)S(1)} %bitcast.41, f32[1,8,16,512]{3,2,1,0:T(8,128)S(1)} %bitcast.37, f32[2,8,16,512]{3,2,1,0:T(8,128)S(1)} %copy-done.1, f32[4,8,16,3]{3,2,1,0:T(8,128)S(1)} %collective-permute-done, ...), kind=kLoop, calls=%fused_computation.36 | loop fusion | flops 1450240 | bytes 2642944 | tf_op jit(solution)/shard_map/sub | solution.py:24
  39.6 0.4 slice_subtract_fusion.1
  40.0 0.2 slice_compare_fusion
  40.2 0.2 slice_multiply_fusion.6
  40.4 0.6 %fusion.16 = f32[2,8,16,513]{3,2,1,0:T(8,128)S(1)} fusion(f32[2,8,16,514]{3,2,1,0:T(8,128)S(1)} %get-tuple-element.11, f32[2,8,16,514]{3,2,1,0:T(8,128)S(1)} %get-tuple-element.10, f32[2,8,16,515]{3,2,1,0:T(8,128)S(1)} %fusion.23, f32[8,16,513]{2,1,0:T(8,128)S(1)} %get-tuple-element.18, f32[8,16,513]{2,1,0:T(8,128)S(1)} %get-tuple-element.17, ...), kind=kLoop, calls=%fused_computation.26 | loop fusion | flops 1313280 | bytes 4005504 | tf_op jit(solution)/shard_map/mul | solution.py:43
  41.0 0.2 fusion.27
  41.2 0.1 fusion.36
  41.3 0.3 collective-permute-start.2
  41.6 4.4 %collective-permute-start.3 = (f32[2,8,16,3]{3,2,1,0:T(8,128)S(1)}, f32[2,8,16,3]{3,2,1,0:T(8,128)S(1)}, u32[]{:S(2)}, u32[]{:S(2)}) collective-permute-start(f32[2,8,16,3]{3,2,1,0:T(8,128)S(1)} %get-tuple-element.13), channel_id=1, source_target_pairs={{4,0},{8,4},{12,8},{16,12},{20,16},{24,20},{28,24},{0,28},{5,1},{9... | collective-permute-start | bytes 9224 | tf_op jit(solution)/shard_map/ppermute | solution.py:16
  46.1 0.8 %pad_maximum_fusion.8 = f32[2,8,16,512]{3,2,1,0:T(8,128)} fusion(f32[1,8,16,512]{3,2,1,0:T(8,128)S(1)} %bitcast.42, f32[1,8,16,512]{3,2,1,0:T(8,128)S(1)} %bitcast.38), kind=kLoop, calls=%fused_computation.53 | loop fusion | flops 131072 | bytes 1048576 | tf_op jit(solution)/shard_map/stack | solution.py:87
  46.9 2.2 %collective-permute-done.2 = f32[2,8,16,3]{3,2,1,0:T(8,128)S(1)} collective-permute-done((f32[2,8,16,3]{3,2,1,0:T(8,128)S(1)}, f32[2,8,16,3]{3,2,1,0:T(8,128)S(1)}, u32[]{:S(2)}, u32[]{:S(2)}) %collective-permute-start.2) | collective-permute-done | bytes 3104 | tf_op jit(solution)/shard_map/ppermute | solution.py:14
  49.1 0.6 %collective-permute-done.3 = f32[2,8,16,3]{3,2,1,0:T(8,128)S(1)} collective-permute-done((f32[2,8,16,3]{3,2,1,0:T(8,128)S(1)}, f32[2,8,16,3]{3,2,1,0:T(8,128)S(1)}, u32[]{:S(2)}, u32[]{:S(2)}) %collective-permute-start.3) | collective-permute-done | bytes 3104 | tf_op jit(solution)/shard_map/ppermute | solution.py:16
  49.7 0.3 pad_maximum_fusion.7
  50.0 0.6 %fusion.11 = f32[2,8,16,515]{3,2,1,0:T(8,128)S(1)} fusion(f32[2,8,16,518]{3,2,1,0:T(8,128)S(1)} %pad_maximum_fusion.7, f32[2,8,16,512]{3,2,1,0:T(8,128)S(1)} %fusion.27, f32[2,8,16,3]{3,2,1,0:T(8,128)S(1)} %collective-permute-done.2, f32[2,8,16,3]{3,2,1,0:T(8,128)S(1)} %collective-permute-done.3), kind=kLoop, calls=%fused_computation.20 | loop fusion | flops 922880 | bytes 2112512 | tf_op jit(solution)/shard_map/sub | solution.py:24
  50.6 0.4 slice_subtract_fusion
  51.0 0.6 %fusion.5 = f32[2,8,16,513]{3,2,1,0:T(8,128)S(1)} fusion(f32[2,8,16,514]{3,2,1,0:T(8,128)S(1)} %get-tuple-element.9, f32[2,8,16,514]{3,2,1,0:T(8,128)S(1)} %get-tuple-element.8, f32[2,8,16,515]{3,2,1,0:T(8,128)S(1)} %fusion.11, f32[8,16,513]{2,1,0:T(8,128)S(1)} %get-tuple-element.18, f32[8,16,513]{2,1,0:T(8,128)S(1)} %get-tuple-element.17, ...), kind=kLoop, calls=%fused_computation.11 | loop fusion | flops 1313280 | bytes 4005504 | tf_op jit(solution)/shard_map/mul | solution.py:43
  51.6 1.0 %fusion.26 = f32[2,8,16,512]{3,2,1,0:T(8,128)} fusion(f32[2,8,16,512]{3,2,1,0:T(8,128)S(1)} %fusion.27, f32[2,8,16,513]{3,2,1,0:T(8,128)S(1)} %fusion.5), kind=kLoop, calls=%fused_computation.50 | loop fusion | flops 262144 | bytes 2097152 | tf_op jit(solution)/shard_map/sub | solution.py:44
  (6 shorter events, 0.1 us)
Async XLA Ops:
  0.6 22.0 %copy-start = (bf16[8,256,512]{2,1,0:T(8,128)(2,1)S(1)}, bf16[8,256,512]{2,1,0:T(8,128)(2,1)}, u32[]{:S(2)}) copy-start(bf16[8,256,512]{2,1,0:T(8,128)(2,1)} %param.11) | copy-start | bytes 6291460
  0.6 10.6 %copy-start.2 = (s32[1,16,8]{1,2,0:T(8,128)S(1)}, s32[1,16,8]{1,2,0:T(8,128)}, u32[]{:S(2)}) copy-start(s32[1,16,8]{1,2,0:T(8,128)} %param.9) | copy-start | bytes 1540
  0.7 10.8 %copy-start.3 = (s32[1,16,8]{1,2,0:T(8,128)S(1)}, s32[1,16,8]{1,2,0:T(8,128)}, u32[]{:S(2)}) copy-start(s32[1,16,8]{1,2,0:T(8,128)} %param.10) | copy-start | bytes 1540
  4.0 16.2 %all-to-all-start = ((bf16[8,4,16,256]{3,2,1,0:T(8,128)(2,1)}), bf16[8,4,16,256]{3,2,1,0:T(8,128)(2,1)S(1)}, u32[]{:S(2)}, u32[]{:S(2)}) async-start(bf16[8,4,16,256]{3,2,1,0:T(8,128)(2,1)} %select_select_fusion), calls=%async_computation | async-start | bytes 524288 | tf_op jit(solution)/shard_map/all_to_all | solution.py:81
  24.5 1.0 %copy-start.1 = (f32[2,8,16,512]{3,2,1,0:T(8,128)S(1)}, f32[2,8,16,512]{3,2,1,0:T(8,128)}, u32[]{:S(2)}) copy-start(f32[2,8,16,512]{3,2,1,0:T(8,128)} %param.6) | copy-start | bytes 1572868
  25.7 10.5 %collective-permute-start = (f32[4,8,16,3]{3,2,1,0:T(8,128)S(1)}, f32[4,8,16,3]{3,2,1,0:T(8,128)S(1)}, u32[]{:S(2)}, u32[]{:S(2)}) collective-permute-start(f32[4,8,16,3]{3,2,1,0:T(8,128)S(1)} %get-tuple-element.6), channel_id=1, source_target_pairs={{0,4},{4,8},{8,12},{12,16},{16,20},{20,24},{24,28},{28,0},{1,5},{5... | collective-permute-start | bytes 18440 | tf_op jit(solution)/shard_map/ppermute | solution.py:14
  27.2 11.3 %collective-permute-start.1 = (f32[4,8,16,3]{3,2,1,0:T(8,128)S(1)}, f32[4,8,16,3]{3,2,1,0:T(8,128)S(1)}, u32[]{:S(2)}, u32[]{:S(2)}) collective-permute-start(f32[4,8,16,3]{3,2,1,0:T(8,128)S(1)} %get-tuple-element.7), channel_id=1, source_target_pairs={{4,0},{8,4},{12,8},{16,12},{20,16},{24,20},{28,24},{0,28},{5,1},{9... | collective-permute-start | bytes 18440 | tf_op jit(solution)/shard_map/ppermute | solution.py:16
  41.3 7.8 %collective-permute-start.2 = (f32[2,8,16,3]{3,2,1,0:T(8,128)S(1)}, f32[2,8,16,3]{3,2,1,0:T(8,128)S(1)}, u32[]{:S(2)}, u32[]{:S(2)}) collective-permute-start(f32[2,8,16,3]{3,2,1,0:T(8,128)S(1)} %get-tuple-element.12), channel_id=1, source_target_pairs={{0,4},{4,8},{8,12},{12,16},{16,20},{20,24},{24,28},{28,0},{1,5},{5... | collective-permute-start | bytes 9224 | tf_op jit(solution)/shard_map/ppermute | solution.py:14
  41.6 8.1 %collective-permute-start.3 = (f32[2,8,16,3]{3,2,1,0:T(8,128)S(1)}, f32[2,8,16,3]{3,2,1,0:T(8,128)S(1)}, u32[]{:S(2)}, u32[]{:S(2)}) collective-permute-start(f32[2,8,16,3]{3,2,1,0:T(8,128)S(1)} %get-tuple-element.13), channel_id=1, source_target_pairs={{4,0},{8,4},{12,8},{16,12},{20,16},{24,20},{28,24},{0,28},{5,1},{9... | collective-permute-start | bytes 9224 | tf_op jit(solution)/shard_map/ppermute | solution.py:16
where the time goes:
time: 52.9 us; the launch traced here: 52.6 us
  waiting for transfers between devices  19.3 us (36%)
  starting transfers between devices  16.8 us (32%)
  other arithmetic  8.56 us (16%)
  local copies, waits for them, and re-layouts  4.72 us (9%)
  matrix products  2.3 us (4%)
  between operations  0.86 us (2%)
    all_to_all x1, waiting for transfers between devices, local(): lax.all_to_all(outgoing, 'tile', split_axis=0, concat_axis=0, tiled=True)  8.56 us
    ppermute x2, waiting for transfers between devices, padded(): lax.ppermute(tail, axis, [(i, (i + 1) % count) for i in range(count)])  7.99 us
    ppermute x2, starting transfers between devices, padded(): lax.ppermute(head, axis, [((i + 1) % count, i) for i in range(count)])  7.75 us
    all_to_all x1, starting transfers between devices, local(): lax.all_to_all(outgoing, 'tile', split_axis=0, concat_axis=0, tiled=True)  7.28 us
    ppermute x2, waiting for transfers between devices, padded(): lax.ppermute(head, axis, [((i + 1) % count, i) for i in range(count)])  2.78 us
    unnamed x10, local copies, waits for them, and re-layouts  1.92 us
    dot_general x1, matrix products, regrid_rows(): jnp.dot(binned, table, preferred_element_type=jnp.float32, precision=lax....  1.83 us
    ppermute x2, starting transfers between devices, padded(): lax.ppermute(tail, axis, [(i, (i + 1) % count) for i in range(count)])  1.8 us
  transfers between devices with their start and end apart: 5, of which 5 were waited for; matrix products, arithmetic and copies ran while one was open for 2% of the time, Pallas kernels for 0%

commit v1 on v0

v1 whole, which is shorter than its diff:
```python
import functools

import jax
import jax.numpy as jnp
from jax import lax
from jax.experimental import pallas as pl
from jax.experimental.pallas import tpu as pltpu
from jax.sharding import PartitionSpec as P

MESH = pl.DeviceIdType.MESH
EDGE = 8
LANES = 128


def substep(q, positive, c_here, c_side, c_cell):
    width = q.shape[-1]

    def at(array, offset):
        return pltpu.roll(array, (-offset) % width, axis=1)

    q_left = at(q, -1)
    edge = (7.0 / 12.0) * (q_left + q) - (1.0 / 12.0) * (at(q, -2) + at(q, 1))
    side = jnp.where(positive, at(edge, -1), at(edge, 1))
    cell = jnp.where(positive, q_left, q)
    flux = c_here * edge + c_side * side + c_cell * cell
    return q - (at(flux, 1) - flux)


def kernel(
    tiles, cap,
    tracer_hbm, met_hbm, list_hbm, entry_hbm, weight_id_hbm, table_hbm,
    next_ref, fields_ref,
    tracer, blocks, lists, entry, kind, table,
    outgoing, arrived, select, raw, turned, halo_q, halo_m,
    load_sem, send_sem, recv_sem, halo_send, halo_recv,
):
    me = lax.axis_index("tile")
    right, left = lax.rem(me + 1, tiles), lax.rem(me + tiles - 1, tiles)
    rows, columns = tracer.shape
    field_rows, cells = blocks.shape[1], blocks.shape[2]
    depth, row_count = entry.shape
    kinds = table.shape[0]
    slots = tiles * cap
    half = rows // 2

    loads = [
        pltpu.make_async_copy(source, target, load_sem.at[i])
        for i, (source, target) in enumerate(
            (
                (list_hbm, lists),
                (met_hbm, blocks),
                (tracer_hbm, tracer),
                (entry_hbm, entry),
                (weight_id_hbm, kind),
                (table_hbm, table),
            )
        )
    ]
    for load in loads:
        load.start()

    barrier = pltpu.get_barrier_semaphore()
    for offset in range(1, tiles):
        pl.semaphore_signal(
            barrier, inc=1, device_id={"tile": lax.rem(me + offset, tiles)}, device_id_type=MESH
        )

    loads[0].wait()
    loads[1].wait()

    def picked(target, slot):
        number = lists[target, me * cap + slot] - me * blocks.shape[0]
        return blocks[jnp.clip(number, 0, blocks.shape[0] - 1)]

    order = sorted(range(1, tiles), key=lambda o: -min(o, tiles - o))
    for offset in order:
        target = lax.rem(me + offset, tiles)
        for slot in range(cap):
            outgoing[offset, slot] = picked(target, slot)

    pl.semaphore_wait(barrier, tiles - 1)
    sends = []
    for offset in order:
        send = pltpu.make_async_remote_copy(
            src_ref=outgoing.at[offset],
            dst_ref=arrived.at[me],
            send_sem=send_sem.at[offset],
            recv_sem=recv_sem.at[offset],
            device_id={"tile": lax.rem(me + offset, tiles)},
            device_id_type=MESH,
        )
        send.start()
        sends.append(send)
    for slot in range(cap):
        arrived[me, slot] = picked(me, slot)

    def exchange(which, halo):
        copies = []
        for i, (span, target) in enumerate(
            ((pl.ds(0, EDGE), left), (pl.ds(LANES - EDGE, EDGE), right))
        ):
            copy = pltpu.make_async_remote_copy(
                src_ref=turned.at[which, span],
                dst_ref=halo.at[span],
                send_sem=halo_send.at[which, i],
                recv_sem=halo_recv.at[which, i],
                device_id={"tile": target},
                device_id_type=MESH,
            )
            copy.start()
            copies.append(copy)
        return copies

    def turn(which, field):
        first = field[:, :LANES].T
        last = field[:, columns - LANES :].T
        turned[which, :EDGE] = first[:EDGE]
        turned[which, LANES - EDGE :] = last[LANES - EDGE :]

    middle = pl.ds(EDGE, LANES - 2 * EDGE)
    halo_q[middle] = jnp.zeros((LANES - 2 * EDGE, rows), jnp.float32)
    halo_m[middle] = jnp.zeros((LANES - 2 * EDGE, rows), jnp.float32)
    loads[2].wait()
    turn(0, tracer)
    sends += exchange(0, halo_q)
    loads[3].wait()
    loads[4].wait()

    key = (kind[...] * slots + entry[...]).T
    width = slots * field_rows
    column = lax.broadcasted_iota(jnp.int32, (row_count, width), 1)
    slot_of = column // field_rows
    field_of = column - slot_of * field_rows
    keys = [jnp.broadcast_to(key[:, k : k + 1], (row_count, width)) for k in range(depth)]
    masks = [
        jnp.where(field_of == f, 1.0, 0.0).astype(jnp.bfloat16) for f in range(field_rows)
    ]
    for w in range(kinds):
        want = slot_of + w * slots
        count = jnp.zeros((row_count, width), jnp.float32)
        for k in range(depth):
            count = count + jnp.where(keys[k] == want, 1.0, 0.0)
        count = count.astype(jnp.bfloat16)
        for f in range(field_rows):
            select[w, pl.ds(f * row_count, row_count), :] = count * masks[f]

    loads[5].wait()
    for send in sends[: tiles - 1]:
        send.wait_recv()

    entries = arrived[...].reshape(width, cells)
    total = jnp.zeros((rows, columns), jnp.float32)
    for w in range(kinds):
        binned = jnp.dot(select[w], entries, preferred_element_type=jnp.float32)
        high = binned.astype(jnp.bfloat16)
        low = (binned - high.astype(jnp.float32)).astype(jnp.bfloat16)
        both = jnp.concatenate([high, low], axis=0)
        product = jnp.dot(both, table[w], preferred_element_type=jnp.float32)
        total = total + (product[:rows] + product[rows:])
    wave = 0.5 * jnp.tanh(total)
    raw[:half] = wave[:half]
    raw[half:] = 1.0 + wave[half:]
    turn(1, raw)
    met_copies = exchange(1, halo_m)
    fields_ref[...] = raw[...]
    for copy in sends[tiles - 1 :]:
        copy.wait_recv()
    q_edges = halo_q[...].T
    for copy in met_copies:
        copy.wait_recv()
    m_edges = halo_m[...].T

    step = 8
    for start in range(0, half, step):
        here = slice(start, start + step)
        there = slice(half + start, half + start + step)
        courant = jnp.concatenate([raw[here], m_edges[here]], axis=1)
        mass = jnp.concatenate([raw[there], m_edges[there]], axis=1)
        size = jnp.abs(courant)
        linear = 0.5 * size
        square = linear * (1.0 - size * (2.0 / 3.0))
        flow = courant * mass
        c_here = flow * (1.0 - linear - 3.0 * square)
        c_side = flow * (linear - 3.0 * square)
        c_cell = flow * (6.0 * square)
        positive = courant > 0
        for span in (here, there):
            q = jnp.concatenate([tracer[span], q_edges[span]], axis=1)
            for _ in range(2):
                q = substep(q, positive, c_here, c_side, c_cell)
            next_ref[span] = q[:, :columns]

    for copy in sends + met_copies:
        copy.wait_send()


def local(tracer, met_blocks, intersection_list, entry_index, weight_id, weight_table):
    tiles = lax.axis_size("tile")
    cap = intersection_list.shape[1] // tiles
    columns = tracer.shape[-1]
    rows = tracer.size // columns
    row_count = entry_index.shape[1]
    field_rows, cells = met_blocks.shape[1:]
    kinds = weight_table.shape[0]
    width = tiles * cap * field_rows
    flat = (rows, columns)
    assert row_count * field_rows == rows
    anywhere = pl.BlockSpec(memory_space=pl.ANY)
    vmem = pl.BlockSpec(memory_space=pltpu.VMEM)
    tracer_next, fields = pl.pallas_call(
        functools.partial(kernel, tiles, cap),
        out_shape=(jax.ShapeDtypeStruct(flat, jnp.float32),) * 2,
        in_specs=[anywhere] * 6,
        out_specs=(vmem, vmem),
        scratch_shapes=[
            pltpu.VMEM(flat, jnp.float32),
            pltpu.VMEM(met_blocks.shape, jnp.bfloat16),
            pltpu.SMEM(intersection_list.shape, jnp.int32),
            pltpu.VMEM(entry_index.shape[:0:-1], jnp.int32),
            pltpu.VMEM(weight_id.shape[:0:-1], jnp.int32),
            pltpu.VMEM(weight_table.shape, jnp.bfloat16),
            pltpu.VMEM((tiles, cap, field_rows, cells), jnp.bfloat16),
            pltpu.VMEM((tiles, cap, field_rows, cells), jnp.bfloat16),
            pltpu.VMEM((kinds, rows, width), jnp.bfloat16),
            pltpu.VMEM(flat, jnp.float32),
            pltpu.VMEM((2, LANES, rows), jnp.float32),
            pltpu.VMEM((LANES, rows), jnp.float32),
            pltpu.VMEM((LANES, rows), jnp.float32),
            pltpu.SemaphoreType.DMA((6,)),
            pltpu.SemaphoreType.DMA((tiles,)),
            pltpu.SemaphoreType.DMA((tiles,)),
            pltpu.SemaphoreType.DMA((2, 2)),
            pltpu.SemaphoreType.DMA((2, 2)),
        ],
        compiler_params=pltpu.CompilerParams(
            collective_id=0, has_side_effects=True, vmem_limit_bytes=60 * 2**20
        ),
        name="regrid_and_advect",
    )(tracer.reshape(flat), met_blocks, intersection_list, entry_index[0].T, weight_id[0].T, weight_table)
    return tracer_next.reshape(tracer.shape), fields.reshape((2,) + tracer.shape[1:])


def solution(mesh):
    return jax.shard_map(
        local,
        mesh=mesh,
        in_specs=(
            P("trc", None, None, "tile"),
            P("tile", None, None),
            P(),
            P("tile", None, None),
            P("tile", None, None),
            P(),
        ),
        out_specs=(P("trc", None, None, "tile"), P(None, None, None, "tile")),
        check_vma=False,
    )
```

time: 52.9 us -> 37.2 us (0.70)
  Pallas kernels: 0 us -> 32.6 us
  waiting for transfers between devices: 19.3 us -> 0 us
  starting transfers between devices: 16.8 us -> 0 us
  other arithmetic: 8.56 us -> 0 us
  matrix products: 2.3 us -> 0 us
  local copies, waits for them, and re-layouts: 4.72 us -> 3.76 us
    pallas_call x0 -> x1, Pallas kernels: none -> 32.6 us  [local(): pl.pallas_call(functools.partial(kernel, tiles, cap), out_shape=(jax.Shap...]
    ppermute x4 -> x0, waiting for transfers between devices: 10.8 us -> none  [the longest x2 7.99 us: padded(): lax.ppermute(tail, axis, [(i, (i + 1) % count) for i in range(count)])]
    ppermute x4 -> x0, starting transfers between devices: 9.55 us -> none  [the longest x2 7.75 us: padded(): lax.ppermute(head, axis, [((i + 1) % count, i) for i in range(count)])]
    all_to_all x1 -> x0, waiting for transfers between devices: 8.56 us -> none  [local(): lax.all_to_all(outgoing, 'tile', split_axis=0, concat_axis=0, tiled=True)]
    all_to_all x1 -> x0, starting transfers between devices: 7.28 us -> none  [local(): lax.all_to_all(outgoing, 'tile', split_axis=0, concat_axis=0, tiled=True)]
    sub x6 -> x0, other arithmetic: 3.23 us -> none  [the longest x2 1.21 us: ppm_substep(): return tracer_ext[..., 3:-3] - (fluxes[..., 1:] - fluxes[..., :-1])]
    dot_general x2 -> x0, matrix products: 2.3 us -> none  [the longest x1 1.83 us: regrid_rows(): jnp.dot(binned, table, preferred_element_type=jnp.float32, precision=lax....]
    gather x2 -> x0, local copies, waits for them, and re-layouts: 2.12 us -> none  [the longest x1 1.47 us: pack_blocks(): picked = jnp.take(blocks, local_ids.reshape(-1), axis=0)]
  transfers between devices with their start and end apart: 5 -> 0, of which waited for: 5 -> 0; matrix products, arithmetic and copies ran while one was open for 2% -> 0% of each run, Pallas kernels for 0% -> 0%
where the time goes in v1:
time: 37.2 us; the launch traced here: 37 us
  Pallas kernels  32.6 us (88%)
  local copies, waits for them, and re-layouts  3.76 us (10%)
  between operations  0.64 us (2%)
    pallas_call x1, Pallas kernels, local(): pl.pallas_call(functools.partial(kernel, tiles, cap), out_shape=(jax.Shap...  32.6 us
    unnamed x2, local copies, waits for them, and re-layouts  3.76 us

profile of v1, /device:TPU:0, one launch (start us, length us, event | category | flops | bytes accessed | tf_op | source)
XLA Modules:
  0.0 37.0 jit_solution(1081167420083178980)
XLA Ops:
  0.6 32.6 %regrid_and_advect.1 = (f32[256,512]{1,0:T(8,128)}, f32[256,512]{1,0:T(8,128)}) custom-call(f32[256,512]{1,0:T(8,128)} %bitcast.11, bf16[16,16,256]{2,1,0:T(8,128)(2,1)} %met_hbm.1, s32[8,32]{1,0:T(8,128)} %list_hbm.1, s32[8,16]{1,0:T(8,128)} %bitcast.12, s32[8,16]{1,0:T(8,128)} %bitcast.13, bf16[8,256,512]{2,1,0:T(8,128)(2,1)} %table_hbm.1), custom_call_target="tpu_custom_call" | custom-call | tf_op jit(solution)/shard_map/regrid_and_advect/pallas_call | solution.py:210
  33.2 1.9 %copy.10 = f32[2,8,16,512]{3,2,1,0:T(8,128)} copy(f32[2,8,16,512]{3,2,1,0:T(8,128)} %bitcast.10) | data formatting | bytes 1048576
  35.1 1.9 %copy.11 = f32[2,8,16,512]{3,2,1,0:T(8,128)} copy(f32[2,8,16,512]{3,2,1,0:T(8,128)} %bitcast.9) | data formatting | bytes 1048576

commit v2 on v1

--- a/solution.py
+++ b/solution.py
@@ -16,7 +16,7 @@
     width = q.shape[-1]
 
     def at(array, offset):
-        return pltpu.roll(array, (-offset) % width, axis=1)
+        return pltpu.roll(array, (-offset) % width, axis=array.ndim - 1)
 
     q_left = at(q, -1)
     edge = (7.0 / 12.0) * (q_left + q) - (1.0 / 12.0) * (at(q, -2) + at(q, 1))
@@ -26,12 +26,58 @@
     return q - (at(flux, 1) - flux)
 
 
+STEP = 64
+
+
+def advect(tracer, raw, q_edges, m_edges, next_hbm, fields_hbm, result, field_sem, store_sem):
+    rows, columns = tracer.shape
+    half = rows // 2
+    fields_copy = pltpu.make_async_copy(raw, fields_hbm, field_sem.at[0])
+    fields_copy.start()
+    copies = []
+    for number, start in enumerate(range(0, half, STEP)):
+        here = slice(start, start + STEP)
+        there = slice(half + start, half + start + STEP)
+        courant = jnp.concatenate([raw[here], m_edges[here]], axis=1)
+        mass = jnp.concatenate([raw[there], m_edges[there]], axis=1)
+        size = jnp.abs(courant)
+        linear = 0.5 * size
+        square = linear * (1.0 - size * (2.0 / 3.0))
+        flow = courant * mass
+        c_here = flow * (1.0 - linear - 3.0 * square)
+        c_side = flow * (linear - 3.0 * square)
+        c_cell = flow * (6.0 * square)
+        positive = courant > 0
+        both = [positive, c_here, c_side, c_cell]
+        both = [jnp.concatenate([one, one], axis=0) for one in both]
+        q = jnp.concatenate(
+            [
+                jnp.concatenate([tracer[span], q_edges[span]], axis=1)
+                for span in (here, there)
+            ],
+            axis=0,
+        )
+        for _ in range(2):
+            q = substep(q, *both)
+        for i, span in enumerate((here, there)):
+            result[span] = q[i * STEP : (i + 1) * STEP, :columns]
+            rows_done = pl.ds(i * half + start, STEP)
+            copy = pltpu.make_async_copy(
+                result.at[rows_done], next_hbm.at[rows_done], store_sem.at[number, i]
+            )
+            copy.start()
+            copies.append(copy)
+    fields_copy.wait()
+    for copy in copies:
+        copy.wait()
+
+
 def kernel(
     tiles, cap,
     tracer_hbm, met_hbm, list_hbm, entry_hbm, weight_id_hbm, table_hbm,
-    next_ref, fields_ref,
-    tracer, blocks, lists, entry, kind, table,
-    outgoing, arrived, select, raw, turned, halo_q, halo_m,
+    tracer, raw, q_edges, m_edges,
+    blocks, lists, entry, kind, table,
+    outgoing, arrived, select, turned, halo_q, halo_m,
     load_sem, send_sem, recv_sem, halo_send, halo_recv,
 ):
     me = lax.axis_index("tile")
@@ -162,33 +208,12 @@
     raw[half:] = 1.0 + wave[half:]
     turn(1, raw)
     met_copies = exchange(1, halo_m)
-    fields_ref[...] = raw[...]
     for copy in sends[tiles - 1 :]:
         copy.wait_recv()
-    q_edges = halo_q[...].T
+    q_edges[...] = halo_q[...].T
     for copy in met_copies:
         copy.wait_recv()
-    m_edges = halo_m[...].T
-
-    step = 8
-    for start in range(0, half, step):
-        here = slice(start, start + step)
-        there = slice(half + start, half + start + step)
-        courant = jnp.concatenate([raw[here], m_edges[here]], axis=1)
-        mass = jnp.concatenate([raw[there], m_edges[there]], axis=1)
-        size = jnp.abs(courant)
-        linear = 0.5 * size
-        square = linear * (1.0 - size * (2.0 / 3.0))
-        flow = courant * mass
-        c_here = flow * (1.0 - linear - 3.0 * square)
-        c_side = flow * (linear - 3.0 * square)
-        c_cell = flow * (6.0 * square)
-        positive = courant > 0
-        for span in (here, there):
-            q = jnp.concatenate([tracer[span], q_edges[span]], axis=1)
-            for _ in range(2):
-                q = substep(q, positive, c_here, c_side, c_cell)
-            next_ref[span] = q[:, :columns]
+    m_edges[...] = halo_m[...].T
 
     for copy in sends + met_copies:
         copy.wait_send()
@@ -205,15 +230,15 @@
     width = tiles * cap * field_rows
     flat = (rows, columns)
     assert row_count * field_rows == rows
-    anywhere = pl.BlockSpec(memory_space=pl.ANY)
+    hbm = pl.BlockSpec(memory_space=pltpu.HBM)
     vmem = pl.BlockSpec(memory_space=pltpu.VMEM)
-    tracer_next, fields = pl.pallas_call(
+    edges = (rows, LANES)
+    held = pl.pallas_call(
         functools.partial(kernel, tiles, cap),
-        out_shape=(jax.ShapeDtypeStruct(flat, jnp.float32),) * 2,
-        in_specs=[anywhere] * 6,
-        out_specs=(vmem, vmem),
+        out_shape=tuple(jax.ShapeDtypeStruct(one, jnp.float32) for one in (flat, flat, edges, edges)),
+        in_specs=[hbm] * 6,
+        out_specs=(vmem,) * 4,
         scratch_shapes=[
-            pltpu.VMEM(flat, jnp.float32),
             pltpu.VMEM(met_blocks.shape, jnp.bfloat16),
             pltpu.SMEM(intersection_list.shape, jnp.int32),
             pltpu.VMEM(entry_index.shape[:0:-1], jnp.int32),
@@ -222,7 +247,6 @@
             pltpu.VMEM((tiles, cap, field_rows, cells), jnp.bfloat16),
             pltpu.VMEM((tiles, cap, field_rows, cells), jnp.bfloat16),
             pltpu.VMEM((kinds, rows, width), jnp.bfloat16),
-            pltpu.VMEM(flat, jnp.float32),
             pltpu.VMEM((2, LANES, rows), jnp.float32),
             pltpu.VMEM((LANES, rows), jnp.float32),
             pltpu.VMEM((LANES, rows), jnp.float32),
@@ -233,10 +257,35 @@
             pltpu.SemaphoreType.DMA((2, 2)),
         ],
         compiler_params=pltpu.CompilerParams(
-            collective_id=0, has_side_effects=True, vmem_limit_bytes=60 * 2**20
+            collective_id=0, has_side_effects=True, vmem_limit_bytes=40 * 2**20
         ),
-        name="regrid_and_advect",
-    )(tracer.reshape(flat), met_blocks, intersection_list, entry_index[0].T, weight_id[0].T, weight_table)
+        name="gather_and_regrid",
+    )(
+        *(
+            pltpu.with_memory_space_constraint(one, pltpu.HBM)
+            for one in (
+                tracer.reshape(flat),
+                met_blocks,
+                intersection_list,
+                entry_index[0].T,
+                weight_id[0].T,
+                weight_table,
+            )
+        )
+    )
+    tracer_next, fields = pl.pallas_call(
+        advect,
+        out_shape=(jax.ShapeDtypeStruct(flat, jnp.float32),) * 2,
+        in_specs=[vmem] * 4,
+        out_specs=(hbm, hbm),
+        scratch_shapes=[
+            pltpu.VMEM(flat, jnp.float32),
+            pltpu.SemaphoreType.DMA((1,)),
+            pltpu.SemaphoreType.DMA((rows // 2 // STEP, 2)),
+        ],
+        compiler_params=pltpu.CompilerParams(vmem_limit_bytes=40 * 2**20),
+        name="advect",
+    )(*held)
     return tracer_next.reshape(tracer.shape), fields.reshape((2,) + tracer.shape[1:])
 
 

time: 37.2 us -> 24.8 us (0.67)
  Pallas kernels: 32.6 us -> 23.9 us
  local copies, waits for them, and re-layouts: 3.76 us -> 0 us
    pallas_call x1 -> x2, Pallas kernels: 32.6 us -> 23.9 us  [the longest x1 20.8 us: local(): pl.pallas_call(functools.partial(kernel, tiles, cap), out_shape=tuple((ja...]
    unnamed x2 -> x0, local copies, waits for them, and re-layouts: 3.76 us -> none
where the time goes in v2:
time: 24.8 us; the launch traced here: 24.6 us
  Pallas kernels  23.9 us (96%)
  between operations  0.64 us (3%)
    pallas_call x1, Pallas kernels, local(): pl.pallas_call(functools.partial(kernel, tiles, cap), out_shape=tuple((ja...  20.8 us
    pallas_call x1, Pallas kernels, local(): pl.pallas_call(advect, out_shape=(jax.ShapeDtypeStruct(flat, jnp.float32)...  3.18 us

profile of v2, /device:TPU:0, one launch (start us, length us, event | category | flops | bytes accessed | tf_op | source)
XLA Modules:
  0.0 24.6 jit_solution(18444721112236610954)
XLA Ops:
  0.6 20.8 %gather_and_regrid.1 = (f32[256,512]{1,0:T(8,128)S(1)}, f32[256,512]{1,0:T(8,128)S(1)}, f32[256,128]{1,0:T(8,128)S(1)}, f32[256,128]{1,0:T(8,128)S(1)}) custom-call(f32[256,512]{1,0:T(8,128)} %bitcast.9, bf16[16,16,256]{2,1,0:T(8,128)(2,1)} %met_hbm.1, s32[8,32]{1,0:T(8,128)} %list_hbm.1, s32[8,16]{1,0:T(8,128)} %bitcast.10, s32[8,16]{1,0:T(8,128)} %bitcast.11, ...), custom_call_target="tpu_custom_call" | custom-call | tf_op jit(solution)/shard_map/gather_and_regrid/pallas_call | solution.py:236
  21.4 3.2 %advect.1 = (f32[256,512]{1,0:T(8,128)}, f32[256,512]{1,0:T(8,128)}) custom-call(f32[256,512]{1,0:T(8,128)S(1)} %get-tuple-element.8.tracer, f32[256,512]{1,0:T(8,128)S(1)} %get-tuple-element.9.raw, f32[256,128]{1,0:T(8,128)S(1)} %get-tuple-element.10.q_edges, f32[256,128]{1,0:T(8,128)S(1)} %get-tuple-element.11.m_edges), custom_call_target="tpu_custom_call" | custom-call | tf_op jit(solution)/shard_map/advect/pallas_call | solution.py:276

commit v3 on v2

--- a/solution.py
+++ b/solution.py
@@ -1,4 +1,5 @@
 import functools
+import math
 
 import jax
 import jax.numpy as jnp
@@ -9,6 +10,8 @@
 
 MESH = pl.DeviceIdType.MESH
 EDGE = 8
+GROUP = 2
+BATCHES = 2
 LANES = 128
 
 
@@ -73,20 +76,23 @@
 
 
 def kernel(
-    tiles, cap,
+    tiles, cap, group, batches,
     tracer_hbm, met_hbm, list_hbm, entry_hbm, weight_id_hbm, table_hbm,
     tracer, raw, q_edges, m_edges,
-    blocks, lists, entry, kind, table,
-    outgoing, arrived, select, turned, halo_q, halo_m,
-    load_sem, send_sem, recv_sem, halo_send, halo_recv,
+    blocks, lists, entry, kind, outer, inner,
+    outgoing, arrived, select, binned, turned, halo_q, halo_m,
+    load_sem, send_sem, recv_sem, pass_send, pass_recv, halo_send, halo_recv,
 ):
     me = lax.axis_index("tile")
+    trc = lax.axis_index("trc")
+    member = lax.rem(trc, group)
     right, left = lax.rem(me + 1, tiles), lax.rem(me + tiles - 1, tiles)
     rows, columns = tracer.shape
     field_rows, cells = blocks.shape[1], blocks.shape[2]
     depth, row_count = entry.shape
-    kinds = table.shape[0]
+    kinds = table_hbm.shape[0] // cells
     slots = tiles * cap
+    share = cap // group
     half = rows // 2
 
     loads = [
@@ -98,18 +104,27 @@
                 (tracer_hbm, tracer),
                 (entry_hbm, entry),
                 (weight_id_hbm, kind),
-                (table_hbm, table),
+                (table_hbm.at[:, pl.ds(0, LANES)], outer.at[:, pl.ds(0, LANES)]),
+                (table_hbm.at[:, pl.ds(columns - LANES, LANES)], outer.at[:, pl.ds(LANES, LANES)]),
+                (table_hbm.at[:, pl.ds(LANES, columns - 2 * LANES)], inner),
             )
         )
     ]
     for load in loads:
         load.start()
+
+    def across(bit):
+        return trc + bit - 2 * bit * lax.rem(member // bit, 2)
+
+    bits = [bit for bit in (2, 1) if bit < group]
 
     barrier = pltpu.get_barrier_semaphore()
     for offset in range(1, tiles):
         pl.semaphore_signal(
             barrier, inc=1, device_id={"tile": lax.rem(me + offset, tiles)}, device_id_type=MESH
         )
+    for bit in bits:
+        pl.semaphore_signal(barrier, inc=1, device_id={"trc": across(bit)}, device_id_type=MESH)
 
     loads[0].wait()
     loads[1].wait()
@@ -121,24 +136,24 @@
     order = sorted(range(1, tiles), key=lambda o: -min(o, tiles - o))
     for offset in order:
         target = lax.rem(me + offset, tiles)
-        for slot in range(cap):
-            outgoing[offset, slot] = picked(target, slot)
-
-    pl.semaphore_wait(barrier, tiles - 1)
-    sends = []
+        for slot in range(share):
+            outgoing[offset, slot] = picked(target, member * share + slot)
+
+    pl.semaphore_wait(barrier, tiles - 1 + len(bits))
+    sends = {}
     for offset in order:
         send = pltpu.make_async_remote_copy(
             src_ref=outgoing.at[offset],
-            dst_ref=arrived.at[me],
+            dst_ref=arrived.at[member, offset],
             send_sem=send_sem.at[offset],
             recv_sem=recv_sem.at[offset],
             device_id={"tile": lax.rem(me + offset, tiles)},
             device_id_type=MESH,
         )
         send.start()
-        sends.append(send)
+        sends[offset] = send
     for slot in range(cap):
-        arrived[me, slot] = picked(me, slot)
+        arrived[slot // share, 0, slot % share] = picked(me, slot)
 
     def exchange(which, halo):
         copies = []
@@ -157,26 +172,30 @@
             copies.append(copy)
         return copies
 
-    def turn(which, field):
-        first = field[:, :LANES].T
-        last = field[:, columns - LANES :].T
-        turned[which, :EDGE] = first[:EDGE]
-        turned[which, LANES - EDGE :] = last[LANES - EDGE :]
+    def turn(which, first, last):
+        turned[which, :EDGE] = first.T[:EDGE]
+        turned[which, LANES - EDGE :] = last.T[LANES - EDGE :]
 
     middle = pl.ds(EDGE, LANES - 2 * EDGE)
     halo_q[middle] = jnp.zeros((LANES - 2 * EDGE, rows), jnp.float32)
     halo_m[middle] = jnp.zeros((LANES - 2 * EDGE, rows), jnp.float32)
     loads[2].wait()
-    turn(0, tracer)
-    sends += exchange(0, halo_q)
+    turn(0, tracer[:, :LANES], tracer[:, columns - LANES :])
+    q_copies = exchange(0, halo_q)
     loads[3].wait()
     loads[4].wait()
 
     key = (kind[...] * slots + entry[...]).T
     width = slots * field_rows
     column = lax.broadcasted_iota(jnp.int32, (row_count, width), 1)
-    slot_of = column // field_rows
-    field_of = column - slot_of * field_rows
+    place = column // field_rows
+    field_of = column - place * field_rows
+    member_of = place // (tiles * share)
+    offset_of = place // share - member_of * tiles
+    source_of = me - offset_of
+    source_of = jnp.where(source_of < 0, source_of + tiles, source_of)
+    within = place - (place // share) * share
+    slot_of = source_of * cap + member_of * share + within
     keys = [jnp.broadcast_to(key[:, k : k + 1], (row_count, width)) for k in range(depth)]
     masks = [
         jnp.where(field_of == f, 1.0, 0.0).astype(jnp.bfloat16) for f in range(field_rows)
@@ -190,38 +209,75 @@
         for f in range(field_rows):
             select[w, pl.ds(f * row_count, row_count), :] = count * masks[f]
 
+    def forward(which, i, bit, region):
+        first, count = batches[i]
+        span = arrived.at[region, pl.ds(first, count)]
+        copy = pltpu.make_async_remote_copy(
+            src_ref=span,
+            dst_ref=span,
+            send_sem=pass_send.at[i, which],
+            recv_sem=pass_recv.at[i, which],
+            device_id={"trc": across(bit)},
+            device_id_type=MESH,
+        )
+        copy.start()
+        passed.append(copy)
+        return copy
+
+    passed, late, crossed = [], [], []
+    for i, (first, count) in enumerate(batches):
+        for offset in range(first, first + count):
+            sends[offset].wait_recv()
+        if group == 4:
+            crossed.append(forward(2, i, 2, member))
+        if group > 1:
+            late.append(forward(0, i, 1, member))
+    if group == 4:
+        for i in range(len(batches)):
+            crossed[i].wait_recv()
+            late.append(forward(1, i, 1, across(2) - trc + member))
+    for copy in late:
+        copy.wait_recv()
+
+    entries = arrived[...].reshape(width, cells)
+    for w in range(kinds):
+        part = jnp.dot(select[w], entries, preferred_element_type=jnp.float32)
+        high = part.astype(jnp.bfloat16)
+        low = (part - high.astype(jnp.float32)).astype(jnp.bfloat16)
+        binned[pl.ds(0, rows), pl.ds(w * cells, cells)] = high
+        binned[pl.ds(rows, rows), pl.ds(w * cells, cells)] = low
+
+    def fields(table):
+        product = jnp.dot(binned[...], table[...], preferred_element_type=jnp.float32)
+        wave = 0.5 * jnp.tanh(product[:rows] + product[rows:])
+        return jnp.concatenate([wave[:half], 1.0 + wave[half:]], axis=0)
+
     loads[5].wait()
-    for send in sends[: tiles - 1]:
-        send.wait_recv()
-
-    entries = arrived[...].reshape(width, cells)
-    total = jnp.zeros((rows, columns), jnp.float32)
-    for w in range(kinds):
-        binned = jnp.dot(select[w], entries, preferred_element_type=jnp.float32)
-        high = binned.astype(jnp.bfloat16)
-        low = (binned - high.astype(jnp.float32)).astype(jnp.bfloat16)
-        both = jnp.concatenate([high, low], axis=0)
-        product = jnp.dot(both, table[w], preferred_element_type=jnp.float32)
-        total = total + (product[:rows] + product[rows:])
-    wave = 0.5 * jnp.tanh(total)
-    raw[:half] = wave[:half]
-    raw[half:] = 1.0 + wave[half:]
-    turn(1, raw)
-    met_copies = exchange(1, halo_m)
-    for copy in sends[tiles - 1 :]:
+    loads[6].wait()
+    ends = fields(outer)
+    turn(1, ends[:, :LANES], ends[:, LANES:])
+    m_copies = exchange(1, halo_m)
+    raw[:, :LANES] = ends[:, :LANES]
+    raw[:, columns - LANES :] = ends[:, LANES:]
+    loads[7].wait()
+    raw[:, LANES : columns - LANES] = fields(inner)
+    for copy in q_copies:
         copy.wait_recv()
     q_edges[...] = halo_q[...].T
-    for copy in met_copies:
+    for copy in m_copies:
         copy.wait_recv()
     m_edges[...] = halo_m[...].T
 
-    for copy in sends + met_copies:
+    for copy in [*sends.values(), *passed, *q_copies, *m_copies]:
         copy.wait_send()
 
 
 def local(tracer, met_blocks, intersection_list, entry_index, weight_id, weight_table):
     tiles = lax.axis_size("tile")
     cap = intersection_list.shape[1] // tiles
+    group = math.gcd(math.gcd(cap, lax.axis_size("trc")), GROUP)
+    cuts = [1 + (tiles - 1) * i // BATCHES for i in range(BATCHES + 1)]
+    batches = [(low, high - low) for low, high in zip(cuts, cuts[1:])]
     columns = tracer.shape[-1]
     rows = tracer.size // columns
     row_count = entry_index.shape[1]
@@ -234,7 +290,7 @@
     vmem = pl.BlockSpec(memory_space=pltpu.VMEM)
     edges = (rows, LANES)
     held = pl.pallas_call(
-        functools.partial(kernel, tiles, cap),
+        functools.partial(kernel, tiles, cap, group, batches),
         out_shape=tuple(jax.ShapeDtypeStruct(one, jnp.float32) for one in (flat, flat, edges, edges)),
         in_specs=[hbm] * 6,
         out_specs=(vmem,) * 4,
@@ -243,16 +299,20 @@
             pltpu.SMEM(intersection_list.shape, jnp.int32),
             pltpu.VMEM(entry_index.shape[:0:-1], jnp.int32),
             pltpu.VMEM(weight_id.shape[:0:-1], jnp.int32),
-            pltpu.VMEM(weight_table.shape, jnp.bfloat16),
-            pltpu.VMEM((tiles, cap, field_rows, cells), jnp.bfloat16),
-            pltpu.VMEM((tiles, cap, field_rows, cells), jnp.bfloat16),
+            pltpu.VMEM((kinds * cells, 2 * LANES), jnp.bfloat16),
+            pltpu.VMEM((kinds * cells, columns - 2 * LANES), jnp.bfloat16),
+            pltpu.VMEM((tiles, cap // group, field_rows, cells), jnp.bfloat16),
+            pltpu.VMEM((group, tiles, cap // group, field_rows, cells), jnp.bfloat16),
             pltpu.VMEM((kinds, rows, width), jnp.bfloat16),
+            pltpu.VMEM((2 * rows, kinds * cells), jnp.bfloat16),
             pltpu.VMEM((2, LANES, rows), jnp.float32),
             pltpu.VMEM((LANES, rows), jnp.float32),
             pltpu.VMEM((LANES, rows), jnp.float32),
-            pltpu.SemaphoreType.DMA((6,)),
+            pltpu.SemaphoreType.DMA((8,)),
             pltpu.SemaphoreType.DMA((tiles,)),
             pltpu.SemaphoreType.DMA((tiles,)),
+            pltpu.SemaphoreType.DMA((len(batches), 3)),
+            pltpu.SemaphoreType.DMA((len(batches), 3)),
             pltpu.SemaphoreType.DMA((2, 2)),
             pltpu.SemaphoreType.DMA((2, 2)),
         ],
@@ -269,7 +329,7 @@
                 intersection_list,
                 entry_index[0].T,
                 weight_id[0].T,
-                weight_table,
+                weight_table.reshape(kinds * cells, columns),
             )
         )
     )

time: 24.8 us -> 21.6 us (0.87)
  Pallas kernels: 23.9 us -> 20.8 us
    pallas_call x1, Pallas kernels: 20.8 us -> 17.6 us  [local(): pl.pallas_call(functools.partial(kernel, tiles, cap, group, batches), out...]
where the time goes in v3:
time: 21.6 us; the launch traced here: 21.4 us
  Pallas kernels  20.8 us (96%)
  between operations  0.64 us (3%)
    pallas_call x1, Pallas kernels, local(): pl.pallas_call(functools.partial(kernel, tiles, cap, group, batches), out...  17.6 us
    pallas_call x1, Pallas kernels, local(): pl.pallas_call(advect, out_shape=(jax.ShapeDtypeStruct(flat, jnp.float32)...  3.18 us

profile of v3, /device:TPU:0, one launch (start us, length us, event | category | flops | bytes accessed | tf_op | source)
XLA Modules:
  0.0 21.4 jit_solution(10977420042206447101)
XLA Ops:
  0.6 17.6 %gather_and_regrid.1 = (f32[256,512]{1,0:T(8,128)S(1)}, f32[256,512]{1,0:T(8,128)S(1)}, f32[256,128]{1,0:T(8,128)S(1)}, f32[256,128]{1,0:T(8,128)S(1)}) custom-call(f32[256,512]{1,0:T(8,128)} %bitcast.11, bf16[16,16,256]{2,1,0:T(8,128)(2,1)} %met_hbm.1, s32[8,32]{1,0:T(8,128)} %list_hbm.1, s32[8,16]{1,0:T(8,128)} %bitcast.12, s32[8,16]{1,0:T(8,128)} %bitcast.13, ...), custom_call_target="tpu_custom_call" | custom-call | tf_op jit(solution)/shard_map/gather_and_regrid/pallas_call | solution.py:292
  18.2 3.2 %advect.1 = (f32[256,512]{1,0:T(8,128)}, f32[256,512]{1,0:T(8,128)}) custom-call(f32[256,512]{1,0:T(8,128)S(1)} %get-tuple-element.8.tracer, f32[256,512]{1,0:T(8,128)S(1)} %get-tuple-element.9.raw, f32[256,128]{1,0:T(8,128)S(1)} %get-tuple-element.10.q_edges, f32[256,128]{1,0:T(8,128)S(1)} %get-tuple-element.11.m_edges), custom_call_target="tpu_custom_call" | custom-call | tf_op jit(solution)/shard_map/advect/pallas_call | solution.py:336

commit v4 on v3

--- a/solution.py
+++ b/solution.py
@@ -15,62 +15,45 @@
 LANES = 128
 
 
-def substep(q, positive, c_here, c_side, c_cell):
-    width = q.shape[-1]
+def coefficients(courant, mass):
+    size = jnp.abs(courant)
+    linear = 0.5 * size
+    square = linear * (1.0 - size * (2.0 / 3.0))
+    flow = courant * mass
+    return (
+        courant > 0,
+        flow * (1.0 - linear - 3.0 * square),
+        flow * (linear - 3.0 * square),
+        flow * (6.0 * square),
+    )
+
+
+def advance(q, positive, c_here, c_side, c_cell, axis):
+    width = q.shape[axis]
 
     def at(array, offset):
-        return pltpu.roll(array, (-offset) % width, axis=array.ndim - 1)
-
-    q_left = at(q, -1)
-    edge = (7.0 / 12.0) * (q_left + q) - (1.0 / 12.0) * (at(q, -2) + at(q, 1))
-    side = jnp.where(positive, at(edge, -1), at(edge, 1))
-    cell = jnp.where(positive, q_left, q)
-    flux = c_here * edge + c_side * side + c_cell * cell
-    return q - (at(flux, 1) - flux)
+        return pltpu.roll(array, (-offset) % width, axis=axis)
+
+    for _ in range(2):
+        q_left = at(q, -1)
+        edge = (7.0 / 12.0) * (q_left + q) - (1.0 / 12.0) * (at(q, -2) + at(q, 1))
+        side = jnp.where(positive, at(edge, -1), at(edge, 1))
+        cell = jnp.where(positive, q_left, q)
+        flux = c_here * edge + c_side * side + c_cell * cell
+        q = q - (at(flux, 1) - flux)
+    return q
 
 
 STEP = 64
 
 
-def advect(tracer, raw, q_edges, m_edges, next_hbm, fields_hbm, result, field_sem, store_sem):
-    rows, columns = tracer.shape
-    half = rows // 2
-    fields_copy = pltpu.make_async_copy(raw, fields_hbm, field_sem.at[0])
-    fields_copy.start()
-    copies = []
-    for number, start in enumerate(range(0, half, STEP)):
-        here = slice(start, start + STEP)
-        there = slice(half + start, half + start + STEP)
-        courant = jnp.concatenate([raw[here], m_edges[here]], axis=1)
-        mass = jnp.concatenate([raw[there], m_edges[there]], axis=1)
-        size = jnp.abs(courant)
-        linear = 0.5 * size
-        square = linear * (1.0 - size * (2.0 / 3.0))
-        flow = courant * mass
-        c_here = flow * (1.0 - linear - 3.0 * square)
-        c_side = flow * (linear - 3.0 * square)
-        c_cell = flow * (6.0 * square)
-        positive = courant > 0
-        both = [positive, c_here, c_side, c_cell]
-        both = [jnp.concatenate([one, one], axis=0) for one in both]
-        q = jnp.concatenate(
-            [
-                jnp.concatenate([tracer[span], q_edges[span]], axis=1)
-                for span in (here, there)
-            ],
-            axis=0,
-        )
-        for _ in range(2):
-            q = substep(q, *both)
-        for i, span in enumerate((here, there)):
-            result[span] = q[i * STEP : (i + 1) * STEP, :columns]
-            rows_done = pl.ds(i * half + start, STEP)
-            copy = pltpu.make_async_copy(
-                result.at[rows_done], next_hbm.at[rows_done], store_sem.at[number, i]
-            )
-            copy.start()
-            copies.append(copy)
-    fields_copy.wait()
+def write(done, raw, next_hbm, fields_hbm, sems):
+    copies = [
+        pltpu.make_async_copy(done, next_hbm, sems.at[0]),
+        pltpu.make_async_copy(raw, fields_hbm, sems.at[1]),
+    ]
+    for copy in copies:
+        copy.start()
     for copy in copies:
         copy.wait()
 
@@ -78,8 +61,8 @@
 def kernel(
     tiles, cap, group, batches,
     tracer_hbm, met_hbm, list_hbm, entry_hbm, weight_id_hbm, table_hbm,
-    tracer, raw, q_edges, m_edges,
-    blocks, lists, entry, kind, outer, inner,
+    done, raw,
+    tracer, blocks, lists, entry, kind, outer, inner,
     outgoing, arrived, select, binned, turned, halo_q, halo_m,
     load_sem, send_sem, recv_sem, pass_send, pass_recv, halo_send, halo_recv,
 ):
@@ -173,12 +156,9 @@
         return copies
 
     def turn(which, first, last):
-        turned[which, :EDGE] = first.T[:EDGE]
-        turned[which, LANES - EDGE :] = last.T[LANES - EDGE :]
-
-    middle = pl.ds(EDGE, LANES - 2 * EDGE)
-    halo_q[middle] = jnp.zeros((LANES - 2 * EDGE, rows), jnp.float32)
-    halo_m[middle] = jnp.zeros((LANES - 2 * EDGE, rows), jnp.float32)
+        turned[which, : 2 * EDGE] = first.T[: 2 * EDGE]
+        turned[which, LANES - 2 * EDGE :] = last.T[LANES - 2 * EDGE :]
+
     loads[2].wait()
     turn(0, tracer[:, :LANES], tracer[:, columns - LANES :])
     q_copies = exchange(0, halo_q)
@@ -261,12 +241,44 @@
     raw[:, columns - LANES :] = ends[:, LANES:]
     loads[7].wait()
     raw[:, LANES : columns - LANES] = fields(inner)
-    for copy in q_copies:
+
+    for start in range(0, half, STEP):
+        here = slice(start, start + STEP)
+        there = slice(half + start, half + start + STEP)
+        factors = [
+            jnp.concatenate([one, one], axis=0) for one in coefficients(raw[here], raw[there])
+        ]
+        q = advance(jnp.concatenate([tracer[here], tracer[there]], axis=0), *factors, 1)
+        done[here] = q[:STEP]
+        done[there] = q[STEP:]
+
+    for copy in [*q_copies, *m_copies]:
         copy.wait_recv()
-    q_edges[...] = halo_q[...].T
-    for copy in m_copies:
-        copy.wait_recv()
-    m_edges[...] = halo_m[...].T
+
+    def stripe(q_stripe, m_stripe):
+        factors = [
+            jnp.concatenate([one, one], axis=1)
+            for one in coefficients(m_stripe[:, :half], m_stripe[:, half:])
+        ]
+        return advance(q_stripe, *factors, 0)[EDGE : 2 * EDGE]
+
+    first, last = stripe(
+        *(
+            jnp.concatenate([halo[LANES - EDGE :], turned[which, : 2 * EDGE]], axis=0)
+            for which, halo in enumerate((halo_q, halo_m))
+        )
+    ), stripe(
+        *(
+            jnp.concatenate([turned[which, LANES - 2 * EDGE :], halo[:EDGE]], axis=0)
+            for which, halo in enumerate((halo_q, halo_m))
+        )
+    )
+    gap = jnp.zeros((LANES - 2 * EDGE, rows), jnp.float32)
+    fixed = jnp.concatenate([first, gap, last], axis=0).T
+    lane = lax.broadcasted_iota(jnp.int32, (rows, LANES), 1)
+    done[:, :LANES] = jnp.where(lane < EDGE, fixed, done[:, :LANES])
+    tail = slice(columns - LANES, columns)
+    done[:, tail] = jnp.where(lane >= LANES - EDGE, fixed, done[:, tail])
 
     for copy in [*sends.values(), *passed, *q_copies, *m_copies]:
         copy.wait_send()
@@ -288,13 +300,13 @@
     assert row_count * field_rows == rows
     hbm = pl.BlockSpec(memory_space=pltpu.HBM)
     vmem = pl.BlockSpec(memory_space=pltpu.VMEM)
-    edges = (rows, LANES)
     held = pl.pallas_call(
         functools.partial(kernel, tiles, cap, group, batches),
-        out_shape=tuple(jax.ShapeDtypeStruct(one, jnp.float32) for one in (flat, flat, edges, edges)),
+        out_shape=tuple(jax.ShapeDtypeStruct(one, jnp.float32) for one in (flat, flat)),
         in_specs=[hbm] * 6,
-        out_specs=(vmem,) * 4,
+        out_specs=(vmem,) * 2,
         scratch_shapes=[
+            pltpu.VMEM(flat, jnp.float32),
             pltpu.VMEM(met_blocks.shape, jnp.bfloat16),
             pltpu.SMEM(intersection_list.shape, jnp.int32),
             pltpu.VMEM(entry_index.shape[:0:-1], jnp.int32),
@@ -334,17 +346,13 @@
         )
     )
     tracer_next, fields = pl.pallas_call(
-        advect,
+        write,
         out_shape=(jax.ShapeDtypeStruct(flat, jnp.float32),) * 2,
-        in_specs=[vmem] * 4,
+        in_specs=[vmem] * 2,
         out_specs=(hbm, hbm),
-        scratch_shapes=[
-            pltpu.VMEM(flat, jnp.float32),
-            pltpu.SemaphoreType.DMA((1,)),
-            pltpu.SemaphoreType.DMA((rows // 2 // STEP, 2)),
-        ],
-        compiler_params=pltpu.CompilerParams(vmem_limit_bytes=40 * 2**20),
-        name="advect",
+        scratch_shapes=[pltpu.SemaphoreType.DMA((2,))],
+        compiler_params=pltpu.CompilerParams(vmem_limit_bytes=16 * 2**20),
+        name="write",
     )(*held)
     return tracer_next.reshape(tracer.shape), fields.reshape((2,) + tracer.shape[1:])
 

time: 21.6 us -> 19.5 us (0.903)
  Pallas kernels: 20.8 us -> 18.6 us
    pallas_call x1, Pallas kernels: 3.18 us -> 0.99 us  [local(): pl.pallas_call(write, out_shape=(jax.ShapeDtypeStruct(flat, jnp.float32),...]
where the time goes in v4:
time: 19.5 us; the launch traced here: 19.3 us
  Pallas kernels  18.6 us (95%)
  between operations  0.64 us (3%)
    pallas_call x1, Pallas kernels, local(): pl.pallas_call(functools.partial(kernel, tiles, cap, group, batches), out...  17.7 us
    pallas_call x1, Pallas kernels, local(): pl.pallas_call(write, out_shape=(jax.ShapeDtypeStruct(flat, jnp.float32),...  0.99 us

profile of v4, /device:TPU:0, one launch (start us, length us, event | category | flops | bytes accessed | tf_op | source)
XLA Modules:
  0.0 19.3 jit_solution(6570958274850301741)
XLA Ops:
  0.6 17.7 %gather_and_regrid.1 = (f32[256,512]{1,0:T(8,128)S(1)}, f32[256,512]{1,0:T(8,128)S(1)}) custom-call(f32[256,512]{1,0:T(8,128)} %bitcast.11, bf16[16,16,256]{2,1,0:T(8,128)(2,1)} %met_hbm.1, s32[8,32]{1,0:T(8,128)} %list_hbm.1, s32[8,16]{1,0:T(8,128)} %bitcast.12, s32[8,16]{1,0:T(8,128)} %bitcast.13, bf16[2048,512]{1,0:T(8,128)(2,1)} %bitcast.10), custom_call_target="tpu_custom_call" | custom-call | tf_op jit(solution)/shard_map/gather_and_regrid/pallas_call | solution.py:303
  18.3 1.0 %write.1 = (f32[256,512]{1,0:T(8,128)}, f32[256,512]{1,0:T(8,128)}) custom-call(f32[256,512]{1,0:T(8,128)S(1)} %get-tuple-element.6.done, f32[256,512]{1,0:T(8,128)S(1)} %get-tuple-element.7.raw), custom_call_target="tpu_custom_call" | custom-call | tf_op jit(solution)/shard_map/write/pallas_call | solution.py:348

commit v5 on v4

--- a/solution.py
+++ b/solution.py
@@ -93,9 +93,6 @@
             )
         )
     ]
-    for load in loads:
-        load.start()
-
     def across(bit):
         return trc + bit - 2 * bit * lax.rem(member // bit, 2)
 
@@ -109,6 +106,9 @@
     for bit in bits:
         pl.semaphore_signal(barrier, inc=1, device_id={"trc": across(bit)}, device_id_type=MESH)
 
+    for load in loads:
+        load.start()
+
     loads[0].wait()
     loads[1].wait()
 
@@ -116,7 +116,7 @@
         number = lists[target, me * cap + slot] - me * blocks.shape[0]
         return blocks[jnp.clip(number, 0, blocks.shape[0] - 1)]
 
-    order = sorted(range(1, tiles), key=lambda o: -min(o, tiles - o))
+    order = sorted(range(1, tiles), key=lambda o: min(o, tiles - o))
     for offset in order:
         target = lax.rem(me + offset, tiles)
         for slot in range(share):
@@ -159,9 +159,6 @@
         turned[which, : 2 * EDGE] = first.T[: 2 * EDGE]
         turned[which, LANES - 2 * EDGE :] = last.T[LANES - 2 * EDGE :]
 
-    loads[2].wait()
-    turn(0, tracer[:, :LANES], tracer[:, columns - LANES :])
-    q_copies = exchange(0, halo_q)
     loads[3].wait()
     loads[4].wait()
 
@@ -216,6 +213,9 @@
         for i in range(len(batches)):
             crossed[i].wait_recv()
             late.append(forward(1, i, 1, across(2) - trc + member))
+    loads[2].wait()
+    turn(0, tracer[:, :LANES], tracer[:, columns - LANES :])
+    q_copies = exchange(0, halo_q)
     for copy in late:
         copy.wait_recv()
 

time: 19.5 us -> 18.8 us (0.964)
  Pallas kernels: 18.6 us -> 18 us
    pallas_call x1, Pallas kernels: 17.7 us -> 17 us  [local(): pl.pallas_call(functools.partial(kernel, tiles, cap, group, batches), out...]
where the time goes in v5:
time: 18.8 us; the launch traced here: 18.7 us
  Pallas kernels  18 us (96%)
  between operations  0.64 us (3%)
    pallas_call x1, Pallas kernels, local(): pl.pallas_call(functools.partial(kernel, tiles, cap, group, batches), out...  17 us
    pallas_call x1, Pallas kernels, local(): pl.pallas_call(write, out_shape=(jax.ShapeDtypeStruct(flat, jnp.float32),...  0.99 us

profile of v5, /device:TPU:0, one launch (start us, length us, event | category | flops | bytes accessed | tf_op | source)
XLA Modules:
  0.0 18.7 jit_solution(9144311340648821546)
XLA Ops:
  0.6 17.0 %gather_and_regrid.1 = (f32[256,512]{1,0:T(8,128)S(1)}, f32[256,512]{1,0:T(8,128)S(1)}) custom-call(f32[256,512]{1,0:T(8,128)} %bitcast.11, bf16[16,16,256]{2,1,0:T(8,128)(2,1)} %met_hbm.1, s32[8,32]{1,0:T(8,128)} %list_hbm.1, s32[8,16]{1,0:T(8,128)} %bitcast.12, s32[8,16]{1,0:T(8,128)} %bitcast.13, bf16[2048,512]{1,0:T(8,128)(2,1)} %bitcast.10), custom_call_target="tpu_custom_call" | custom-call | tf_op jit(solution)/shard_map/gather_and_regrid/pallas_call | solution.py:303
  17.7 1.0 %write.1 = (f32[256,512]{1,0:T(8,128)}, f32[256,512]{1,0:T(8,128)}) custom-call(f32[256,512]{1,0:T(8,128)S(1)} %get-tuple-element.6.done, f32[256,512]{1,0:T(8,128)S(1)} %get-tuple-element.7.raw), custom_call_target="tpu_custom_call" | custom-call | tf_op jit(solution)/shard_map/write/pallas_call | solution.py:348
